TPU v7x, 128 devices: a whole 4x4x4 slice. The times are simulated.
128 devices in a mesh: tm: 4 (over y_lo, core), space: 32 (over x, z, y_hi).
Axes of the slice: x: 4, y: 4 (y_hi: 2, y_lo: 2; y = y_hi * 2 + y_lo), z: 4, core: 2. Of those that a mesh axis runs over, the one named last changes fastest.
Arguments:
- departures: float32 [8, 32, 256, 512], P('tm', None, 'space'), may hold values from -6 to 6
- innovations: float32 [524288], P(('tm', 'space')), may hold values from -6 to 6
- obs_variance: float32 [524288], P(('tm', 'space')), may hold values from 0.5 to 2
- dual_state: float32 [8, 32, 256, 512], P('tm', None, 'space'), may hold values from -6 to 6
- obs_dual: float32 [524288], P(('tm', 'space')), may hold values from -6 to 6
- increment: float32 [8, 32, 256, 512], P('tm', None, 'space'), may hold values from -6 to 6
- trajectory: float32 [8, 32, 256, 512], P('tm', None, 'space'), may hold values from -6 to 6
- lat_mix: float32 [256, 256], replicated, may hold values from -0.375 to 0.375
- spectrum: float32 [257], replicated, may hold values from 0.1 to 1
- error_scale: float32 [8], P('tm'), may hold values from 0.3 to 1
- obs_time: int32 [524288], P(('tm', 'space')), may hold values from 0 to 7, as said below
- obs_level: int32 [524288], P(('tm', 'space')), may hold values from 0 to 31
- obs_point: int32 [524288], P(('tm', 'space')), may hold values from 0 to 131071, as said below
Outputs:
- dual_next: float32 [8, 32, 256, 512], P('tm', None, 'space')
- obs_dual_next: float32 [524288], P(('tm', 'space'))
- increment_next: float32 [8, 32, 256, 512], P('tm', None, 'space')
- trajectory_next: float32 [8, 32, 256, 512], P('tm', None, 'space')
Inputs may be any that keep to these rules, and one draw needn't show every extreme that they name: `obs_time`: observations come in blocks of 4096; block b lies in the sub-windows (b // number of latitude bands) * 2 to that plus 2 - 1. `obs_point`: block b of 4096 observations lies in the latitudes (b mod number of latitude bands) * 8 to that plus 8 - 1.
All inputs are finite; a program needn't handle non-finite values.
Results may differ from a plain program's by a relative error of at most 0.0001.
Values sent between devices are 32-bit elements; how exact they have to be, the bound alone decides.
A program may use at most 128 MiB of HBM per device.

v0:
```python
import functools
import math

import jax
import jax.numpy as jnp
import numpy as np
from jax import lax
from jax.experimental import pallas as pl
from jax.experimental.pallas import tpu as pltpu
from jax.sharding import PartitionSpec as P

MESH = pl.DeviceIdType.MESH
ROWS = 8
GROUP = 4
F32 = jnp.float32
BF16 = jnp.bfloat16
SINE = (-2.5052108385e-8, 2.7557319224e-6, -1.9841269841e-4, 8.3333333333e-3, -1.6666666667e-1)


def sine(angle):
    turns = jnp.floor(angle * (1.0 / math.pi) + 0.5)
    rest = angle - turns * 3.140625
    rest = rest - turns * 9.67653589793e-4
    square = rest * rest
    series = SINE[0]
    for factor in SINE[1:]:
        series = series * square + factor
    half = turns * 0.5
    sign = 1.0 - 4.0 * (half - jnp.floor(half))
    return sign * (rest + rest * square * series)


def split(values):
    high = values.astype(BF16)
    return high, (values - high.astype(F32)).astype(BF16)


def dot(left, right, dims=((1,), (0,))):
    return lax.dot_general(left, right, (dims, ((), ())), preferred_element_type=F32)


def kernel(
    groups,
    bands,
    base_ref,
    mix_ref,
    scale_ref,
    dep,
    dual,
    incr,
    traj,
    innov,
    variance,
    held,
    time_ref,
    level_ref,
    point_ref,
    out_dual,
    out_held,
    out_incr,
    out_slid,
    east,
    north,
    zonal_hi,
    zonal_lo,
    mix_hi,
    mix_lo,
    row_ref,
    lon_ref,
    row_table,
    spread_ref,
    turned_hi,
    turned_lo,
    held1,
    dual1,
    pulled,
    pull_send,
    pull_recv,
    prior,
    incr1,
    part,
    slid_send,
    fore1,
    fore2,
    mixed1,
    mixed2,
    back1,
    back2,
    halo_send,
    halo_recv,
    far_send,
    far_recv,
    pull_ssem,
    pull_rsem,
    prior_ssem,
    prior_rsem,
    slid_ssem,
    slid_rsem,
    halo_ssem,
    halo_rsem,
):
    windows, levels, _, width = dep.shape
    obs = innov.shape[1]
    cells = windows * levels * ROWS
    chunk = min(512, obs)
    me = lax.axis_index("space")
    grp = lax.axis_index("tm")
    has_prev, has_next = grp > 0, grp < groups - 1
    has_below, has_above = me > 0, me < bands - 1
    line = lax.broadcasted_iota(jnp.int32, (ROWS, width), 0)
    is_first, is_last = line == 0, line == ROWS - 1

    def both(*flags):
        return functools.reduce(jnp.logical_and, flags)

    barrier = pltpu.get_barrier_semaphore()
    around = ((0, None), (-1, has_below), (1, has_above))

    def greet(j, carry):
        pl.semaphore_signal(barrier, inc=1, device_id=(grp, lax.rem(me + j, bands)), device_id_type=MESH)
        return carry

    lax.fori_loop(1, bands, greet, 0)
    for shift, there in ((-1, has_prev), (1, has_next)):
        for step, beside in around:
            flags = [there] if beside is None else [there, beside]

            @pl.when(both(*flags))
            def _(shift=shift, step=step):
                pl.semaphore_signal(barrier, inc=1, device_id=(grp + shift, me + step), device_id_type=MESH)

    def await_barrier():
        beside = 1 + has_below.astype(jnp.int32) + has_above.astype(jnp.int32)
        other = has_prev.astype(jnp.int32) + has_next.astype(jnp.int32)
        pl.semaphore_wait(barrier, bands - 1 + other * beside)

    def remote(source, target, ssem, rsem, device):
        return pltpu.make_async_remote_copy(
            src_ref=source, dst_ref=target, send_sem=ssem, recv_sem=rsem, device_id=device, device_id_type=MESH
        )

    def each_level(body):
        def step(i, carry):
            for u in range(GROUP):
                body(i * GROUP + u)
            return carry

        lax.fori_loop(0, levels // GROUP, step, 0)

    def rows_of(j):
        return pl.ds(pl.multiple_of(j * ROWS, ROWS), ROWS)

    def send_out(source, target, k, s):
        def step(j, carry):
            to = lax.rem(me + j, bands)
            remote(source.at[s, to], target.at[s, rows_of(me)], far_send.at[k, s], far_recv.at[k, s], (grp, to)).start()
            return carry

        lax.fori_loop(1, bands, step, 0)
        target[s, rows_of(me), :] = source[s, me]

    def send_back(source, target, k, s):
        def step(j, carry):
            to = lax.rem(me + j, bands)
            remote(source.at[s, rows_of(to)], target.at[s, me], far_send.at[k, s], far_recv.at[k, s], (grp, to)).start()
            return carry

        lax.fori_loop(1, bands, step, 0)
        target[s, me] = source[s, rows_of(me), :]

    def all_but_one(ref, s):
        return ref.at[s, pl.ds(0, bands - 1)] if ref.ndim == 4 else ref.at[s, pl.ds(0, (bands - 1) * ROWS)]

    def far_copy(source, target, k, s):
        return remote(all_but_one(source, s), all_but_one(target, s), far_send.at[k, s], far_recv.at[k, s], (grp, me))

    def halo(phase, way, s):
        pulls = phase < 2
        to_group = (grp - 1 if pulls else grp) if s == 0 else (grp if pulls else grp + 1)
        to_band = me + 1 if way == 0 else me - 1
        return remote(
            halo_send.at[phase, way, s],
            halo_recv.at[phase, way, 1 - s],
            halo_ssem.at[phase, way, s],
            halo_rsem.at[phase, way, 1 - s],
            (to_group, to_band),
        )

    def halo_sends(phase, way, s):
        beside = has_above if way == 0 else has_below
        if phase < 2 and s == 0:
            return both(beside, has_prev)
        if phase >= 2 and s == 1:
            return both(beside, has_next)
        return beside

    def halo_hears(phase, way, s):
        beside = has_below if way == 0 else has_above
        if phase < 2 and s == 1:
            return both(beside, has_next)
        if phase >= 2 and s == 0:
            return both(beside, has_prev)
        return beside

    def halo_start(phase, s):
        for way in (0, 1):

            @pl.when(halo_sends(phase, way, s))
            def _(way=way):
                halo(phase, way, s).start()

    def halo_wait(phase, s):
        for way in (0, 1):

            @pl.when(halo_hears(phase, way, s))
            def _(way=way):
                halo(phase, way, 1 - s).wait_recv()

            @pl.when(jnp.logical_not(halo_hears(phase, way, s)))
            def _(way=way):
                halo_recv[phase, way, s] = jnp.zeros((levels, width), F32)

    def halo_row(phase, way, s, lev):
        return halo_recv[phase, way, s, pl.ds(lev, 1), :]

    def pull_copy(k):
        return remote(pull_send.at[k], pull_recv.at[k], pull_ssem.at[k], pull_rsem.at[k], (grp - 1, me))

    def prior_copy(k, source):
        return remote(source.at[1], prior.at[k], prior_ssem.at[k], prior_rsem.at[k], (grp + 1, me))

    def hear_next(copy, buffer):
        @pl.when(has_next)
        def _():
            copy.wait_recv()

        @pl.when(jnp.logical_not(has_next))
        def _():
            buffer[...] = jnp.zeros(buffer.shape, F32)

    def hear_prev(copy, buffer):
        @pl.when(has_prev)
        def _():
            copy.wait_recv()

        @pl.when(jnp.logical_not(has_prev))
        def _():
            buffer[...] = jnp.zeros(buffer.shape, F32)

    def pull(phase, s, lev, field):
        pe, pn = east[s, lev], north[s, lev]
        down = field * pn
        up = field * (0.2 - pn)
        halo_send[phase, 0, s, pl.ds(lev, 1), :] = up[ROWS - 1 :, :]
        halo_send[phase, 1, s, pl.ds(lev, 1), :] = down[:1, :]
        return (
            0.6 * field
            + pltpu.roll(field * pe, width - 1, 1)
            + pltpu.roll(field * (0.2 - pe), 1, 1)
            + jnp.where(is_last, 0.0, pltpu.roll(down, ROWS - 1, 0))
            + jnp.where(is_first, 0.0, pltpu.roll(up, 1, 0))
        )

    def pulled_halo(phase, s, lev):
        return jnp.where(is_first, halo_row(phase, 0, s, lev), 0.0) + jnp.where(is_last, halo_row(phase, 1, s, lev), 0.0)

    def push(phase, s, lev, field):
        pe, pn = east[s, lev], north[s, lev]
        above = jnp.where(is_last, halo_row(phase, 1, s, lev), pltpu.roll(field, ROWS - 1, 0))
        below = jnp.where(is_first, halo_row(phase, 0, s, lev), pltpu.roll(field, 1, 0))
        return (
            0.6 * field
            + pltpu.roll(field, width - 1, 1) * (0.2 - pe)
            + pltpu.roll(field, 1, 1) * pe
            + above * (0.2 - pn)
            + below * pn
        )

    def edge_rows(phase, s, lev, field):
        halo_send[phase, 0, s, pl.ds(lev, 1), :] = field[ROWS - 1 :, :]
        halo_send[phase, 1, s, pl.ds(lev, 1), :] = field[:1, :]

    def piece(c):
        return pl.ds(pl.multiple_of(c * chunk, chunk), chunk)

    def tables():
        shift = width.bit_length() - 1
        point = point_ref[...]
        row_ref[...] = ((time_ref[...] - grp * windows) * levels + level_ref[...]) * ROWS + (
            lax.shift_right_logical(point, shift) - me * ROWS
        )
        lon_ref[...] = jnp.bitwise_and(point, width - 1)

        def step(c, carry):
            wanted = row_ref[:, piece(c)]
            block = 64
            for r in range(0, cells, block):
                spot = lax.broadcasted_iota(jnp.int32, (block, chunk), 0) + r
                row_table[r : r + block, piece(c)] = jnp.where(spot == wanted, 1.0, 0.0).astype(BF16)
            return carry

        lax.fori_loop(0, obs // chunk, step, 0)

    def spread(values):
        spread_ref[...] = jnp.zeros(spread_ref.shape, F32)

        def step(c, carry):
            weight = values[:, piece(c)]
            high = weight.astype(BF16).astype(F32)
            low = weight - high
            hit = lax.broadcasted_iota(jnp.int32, (width, chunk), 0) == lon_ref[:, piece(c)]
            chosen = row_table[:, piece(c)]
            total = dot(chosen, jnp.where(hit, high, 0.0).astype(BF16), ((1,), (1,)))
            total = total + dot(chosen, jnp.where(hit, low, 0.0).astype(BF16), ((1,), (1,)))
            spread_ref[...] += total
            return carry

        lax.fori_loop(0, obs // chunk, step, 0)

    def observe(state, old, new):
        turned = state[...].reshape(cells, width).T
        turned_hi[...], turned_lo[...] = split(turned)

        def step(c, carry):
            chosen = row_table[:, piece(c)]
            picked = dot(turned_hi[...], chosen) + dot(turned_lo[...], chosen)
            hit = lax.broadcasted_iota(jnp.int32, (width, chunk), 0) == lon_ref[:, piece(c)]
            seen = jnp.sum(jnp.where(hit, picked, 0.0), axis=0, keepdims=True)
            spread_of, before = variance[:, piece(c)], old[:, piece(c)]
            new[:, piece(c)] = before + (innov[:, piece(c)] - spread_of * before - seen) / spread_of
            return carry

        lax.fori_loop(0, obs // chunk, step, 0)

    def cover(source, target, s):
        high, low = split(source[s])
        smooth = dot(high, zonal_hi[...]) + (dot(high, zonal_lo[...]) + dot(low, zonal_hi[...]))
        high, low = split(smooth)
        mixed = smooth + (dot(mix_hi[...], high) + (dot(mix_hi[...], low) + dot(mix_lo[...], high)))
        scale = scale_ref[s]
        target[s] = mixed * (scale * scale)

    def first(lev):
        for s in (0, 1):
            wind = traj[s, lev]
            east[s, lev] = 0.1 + 0.25 * jnp.tanh(wind)
            north[s, lev] = 0.1 + 0.25 * sine(wind)
            value = pull(0, s, lev, dual[s, lev])
            if s == 0:
                pull_send[0, lev] = value
            else:
                pulled[lev] = value
            edge_rows(2, s, lev, incr[s, lev])

    each_level(first)
    await_barrier()

    @pl.when(has_prev)
    def _():
        pull_copy(0).start()

    for s in (1, 0):
        halo_start(0, s)

    @pl.when(has_next)
    def _():
        prior_copy(0, incr).start()

    for s in (0, 1):
        halo_start(2, s)

    tables()
    spread(held)

    def circulant(a, carry):
        tall = [pltpu.roll(base_ref[...], a * 16 + t, 1) for t in (0, 8)]
        high, low = split(jnp.concatenate(tall, axis=0))
        at = pl.ds(pl.multiple_of(a * 16, 16), 16)
        zonal_hi[at, :] = high
        zonal_lo[at, :] = low
        return carry

    halo_wait(0, 0)

    def dual1_here(lev):
        field = pulled[lev] + pulled_halo(0, 0, lev) - spread_ref[rows_of(lev), :]
        dual1[0, lev] = field
        pull_send[1, lev] = pull(1, 0, lev, field)

    each_level(dual1_here)
    send_out(dual1, fore1, 0, 0)

    @pl.when(has_prev)
    def _():
        pull_copy(1).start()

    halo_start(1, 0)
    hear_next(pull_copy(0), pull_recv.at[0])
    halo_wait(0, 1)

    def dual1_next(lev):
        field = pull_recv[0, lev] + pulled_halo(0, 1, lev) - spread_ref[rows_of(levels + lev), :]
        dual1[1, lev] = field
        pulled[lev] = pull(1, 1, lev, field)

    each_level(dual1_next)
    send_out(dual1, fore1, 0, 1)
    halo_start(1, 1)

    lax.fori_loop(0, width // 16, circulant, 0)
    mix_hi[...], mix_lo[...] = split(mix_ref[...])
    observe(incr, held, held1)
    spread(held1)
    halo_wait(1, 0)

    def dual2_here(lev):
        out_dual[0, lev] = pulled[lev] + pulled_halo(1, 0, lev) - spread_ref[rows_of(lev), :]

    each_level(dual2_here)
    send_out(out_dual, fore2, 1, 0)
    hear_next(pull_copy(1), pull_recv.at[1])
    halo_wait(1, 1)

    def dual2_next(lev):
        out_dual[1, lev] = pull_recv[1, lev] + pulled_halo(1, 1, lev) - spread_ref[rows_of(levels + lev), :]

    each_level(dual2_next)
    send_out(out_dual, fore2, 1, 1)

    for s in (0, 1):
        far_copy(dual1, fore1, 0, s).wait_recv()
        cover(fore1, mixed1, s)
        send_back(mixed1, back1, 2, s)

    hear_prev(prior_copy(0, incr), prior.at[0])
    halo_wait(2, 0)
    halo_wait(2, 1)

    def moved1(lev):
        part[0, lev] = dep[0, lev] + push(2, 0, lev, prior[0, lev])
        part[1, lev] = dep[1, lev] + push(2, 1, lev, incr[0, lev])

    each_level(moved1)

    for s in (0, 1):
        far_copy(out_dual, fore2, 1, s).wait_recv()
        cover(fore2, mixed2, s)
        send_back(mixed2, back2, 3, s)

    for s in (1, 0):
        far_copy(mixed1, back1, 2, s).wait_recv()

        def incr1_of(lev, s=s):
            field = part[s, lev] - back1[s, lev]
            incr1[s, lev] = field
            edge_rows(3, s, lev, field)

        each_level(incr1_of)
        if s == 1:

            @pl.when(has_next)
            def _():
                prior_copy(1, incr1).start()

        halo_start(3, s)

    observe(incr1, held1, out_held)

    def finish(s, lev, before):
        field = dep[s, lev] + push(3, s, lev, before) - back2[s, lev]
        out_incr[s, lev] = field
        slid_send[s, lev] = traj[s, lev] + field

    def slid_copy(s):
        return remote(slid_send.at[s], out_slid.at[s], slid_ssem.at[s], slid_rsem.at[s], (grp - 1, me))

    for s in (1, 0):
        if s == 0:
            hear_prev(prior_copy(1, incr1), prior.at[1])
        halo_wait(3, s)
        far_copy(mixed2, back2, 3, s).wait_recv()
        each_level(lambda lev, s=s: finish(s, lev, prior[1, lev] if s == 0 else incr1[0, lev]))

        @pl.when(has_prev)
        def _(s=s):
            slid_copy(s).start()

    @pl.when(jnp.logical_not(has_next))
    def _():
        def stay(lev):
            for s in (0, 1):
                out_slid[s, lev] = slid_send[1, lev]

        each_level(stay)

    for s in (0, 1):

        @pl.when(has_next)
        def _(s=s):
            slid_copy(s).wait_recv()

    for s in (0, 1):
        far_copy(dual1, fore1, 0, s).wait_send()
        far_copy(out_dual, fore2, 1, s).wait_send()
        far_copy(mixed1, back1, 2, s).wait_send()
        far_copy(mixed2, back2, 3, s).wait_send()
    for phase in range(4):
        for way in (0, 1):
            for s in (0, 1):

                @pl.when(halo_sends(phase, way, s))
                def _(phase=phase, way=way, s=s):
                    halo(phase, way, s).wait_send()

    @pl.when(has_prev)
    def _():
        pull_copy(0).wait_send()
        pull_copy(1).wait_send()
        slid_copy(0).wait_send()
        slid_copy(1).wait_send()

    @pl.when(has_next)
    def _():
        prior_copy(0, incr).wait_send()
        prior_copy(1, incr1).wait_send()


def circulant_rows(spectrum, width):
    modes, cells = np.arange(width // 2 + 1), np.arange(width)
    weight = np.where((modes == 0) | (modes == width // 2), 1.0, 2.0) / width
    angle = (modes[:, None] * cells[None, :] % width) * (2.0 * math.pi / width)
    table = jnp.asarray((np.cos(angle) * weight[:, None]).astype(np.float32))
    response = jnp.sum(table * spectrum[:, None], axis=0)
    return jnp.stack([jnp.roll(response, i) for i in range(ROWS)])


def on_device(
    departures,
    innovations,
    obs_variance,
    dual_state,
    obs_dual,
    increment,
    trajectory,
    lat_mix,
    spectrum,
    error_scale,
    obs_time,
    obs_level,
    obs_point,
):
    groups, bands = lax.axis_size("tm"), lax.axis_size("space")
    windows, levels, rows, width = increment.shape
    lats = bands * rows
    obs = obs_dual.shape[0]
    cells = windows * levels * rows
    base = circulant_rows(spectrum, width)
    flat = [v.reshape(1, obs) for v in (innovations, obs_variance, obs_dual, obs_time, obs_level, obs_point)]
    state = jax.ShapeDtypeStruct(increment.shape, F32)
    vmem = pl.BlockSpec(memory_space=pltpu.VMEM)
    whole = pltpu.VMEM(increment.shape, F32)
    pencil = pltpu.VMEM((windows, lats, width), F32)
    window = pltpu.VMEM((levels, rows, width), F32)
    window2 = pltpu.VMEM((2, levels, rows, width), F32)
    edge = pltpu.VMEM((4, 2, 2, levels, width), F32)
    dma = pltpu.SemaphoreType.DMA
    dual, held, incr, slid = pl.pallas_call(
        functools.partial(kernel, groups, bands),
        out_shape=(state, jax.ShapeDtypeStruct((1, obs), F32), state, state),
        in_specs=[vmem, vmem, pl.BlockSpec(memory_space=pltpu.SMEM)] + [vmem] * 10,
        out_specs=(vmem,) * 4,
        scratch_shapes=[
            whole,
            whole,
            pltpu.VMEM((width, width), BF16),
            pltpu.VMEM((width, width), BF16),
            pltpu.VMEM((lats, lats), BF16),
            pltpu.VMEM((lats, lats), BF16),
            pltpu.VMEM((1, obs), jnp.int32),
            pltpu.VMEM((1, obs), jnp.int32),
            pltpu.VMEM((cells, obs), BF16),
            pltpu.VMEM((cells, width), F32),
            pltpu.VMEM((width, cells), BF16),
            pltpu.VMEM((width, cells), BF16),
            pltpu.VMEM((1, obs), F32),
            whole,
            window,
            window2,
            window2,
            window2,
            whole,
            whole,
            whole,
            pencil,
            pencil,
            pencil,
            pencil,
            whole,
            whole,
            edge,
            edge,
            dma((4, 2)),
            dma((4, 2)),
            dma((2,)),
            dma((2,)),
            dma((2,)),
            dma((2,)),
            dma((2,)),
            dma((2,)),
            dma((4, 2, 2)),
            dma((4, 2, 2)),
        ],
        compiler_params=pltpu.CompilerParams(
            collective_id=0, has_side_effects=True, vmem_limit_bytes=56 * 1024 * 1024
        ),
    )(
        base,
        lat_mix,
        error_scale,
        departures,
        dual_state,
        increment,
        trajectory,
        *flat,
    )
    return (dual, held.reshape(obs), incr, slid)


def solution(mesh):
    state = P("tm", None, "space", None)
    flat = P(("tm", "space"))
    placed = (state, flat, flat, state, flat, state, state, P(), P(), P("tm"), flat, flat, flat)
    return jax.shard_map(
        on_device,
        mesh=mesh,
        in_specs=placed,
        out_specs=(state, flat, state, state),
        check_vma=False,
    )
```

profile of v0, /device:TPU:1, one launch (start us, length us, event | category | flops | bytes accessed | tf_op | source)
XLA Modules:
  0.0 120.2 jit_solution(6008546390901517059)
XLA Ops:
  0.6 0.0 copy-start.3
  0.6 0.7 copy-done.3
  1.3 1.2 multiply_reduce_fusion
  2.5 0.6 slice.56
  3.1 0.1 slice.68
  3.1 0.1 slice.66
  3.2 0.1 slice.64
  3.3 0.1 slice.62
  3.4 0.1 slice.60
  3.4 0.1 slice.58
  3.5 0.1 pad_maximum_fusion.1
  3.6 0.1 pad_maximum_fusion.2
  3.7 0.1 pad_maximum_fusion.3
  3.7 0.1 pad_maximum_fusion.4
  3.8 0.1 pad_maximum_fusion.5
  3.9 0.1 pad_maximum_fusion.6
  4.0 0.7 pad_maximum_fusion
  4.7 0.6 stack.35.base_ref
  5.3 109.3 %shard_map.165 = (f32[2,32,8,512]{3,2,1,0:T(8,128)}, f32[1,4096]{1,0:T(1,128)}, f32[2,32,8,512]{3,2,1,0:T(8,128)}, f32[2,32,8,512]{3,2,1,0:T(8,128)}) custom-call(f32[8,512]{1,0:T(8,128)} %stack.35.base_ref, f32[256,256]{1,0:T(8,128)} %mix_ref.1, f32[2]{0:T(128)} %scale_ref.1, f32[2,32,8,512]{3,2,1,0:T(8,128)} %dep.1, f32[2,32,8,512]{3,2,1,0:T(8,128)} %dual.1, ...), custom_call_target="tpu_custom_call" | custom-call | tf_op jit(solution)/shard_map/pallas_call | solution.py:567
  114.7 0.0 copy-start.2
  114.7 0.0 copy-start.1
  114.7 2.4 %copy.22 = f32[2,32,8,512]{3,2,1,0:T(8,128)} copy(f32[2,32,8,512]{3,2,1,0:T(8,128)} %get-tuple-element.16) | data formatting | bytes 2097152
  117.0 0.0 copy-done.2
  117.0 0.6 copy.23
  117.6 0.0 copy-done.1
  117.6 0.0 copy-start
  117.7 1.0 copy.24
  118.6 0.6 copy-done
  119.3 1.0 copy.25
Async XLA Ops:
  0.6 0.7 copy-start.3
  114.7 2.4 %copy-start.2 = (f32[1,4096]{1,0:T(1,128)S(1)}, f32[1,4096]{1,0:T(1,128)}, u32[]{:S(2)}) copy-start(f32[1,4096]{1,0:T(1,128)} %get-tuple-element.9) | copy-start | bytes 49156
  114.7 3.0 %copy-start.1 = (f32[2,32,8,512]{3,2,1,0:T(8,128)S(1)}, f32[2,32,8,512]{3,2,1,0:T(8,128)}, u32[]{:S(2)}) copy-start(f32[2,32,8,512]{3,2,1,0:T(8,128)} %get-tuple-element.18) | copy-start | bytes 3145732
  117.6 1.6 %copy-start = (f32[2,32,8,512]{3,2,1,0:T(8,128)S(1)}, f32[2,32,8,512]{3,2,1,0:T(8,128)}, u32[]{:S(2)}) copy-start(f32[2,32,8,512]{3,2,1,0:T(8,128)} %get-tuple-element.19) | copy-start | bytes 3145732
where the time goes:
time: 120 us
  Pallas kernels  109 us (91%)
  local copies, waits for them, and re-layouts  7.87 us (7%)
  other arithmetic  2.33 us (2%)
    pallas_call x1, Pallas kernels, on_device(): pl.pallas_call(functools.partial(kernel, groups, bands), out_shape=(state...  109 us
    unnamed x12, local copies, waits for them, and re-layouts  6.21 us

commit v1 on v0

--- a/solution.py
+++ b/solution.py
@@ -42,23 +42,32 @@
 def kernel(
     groups,
     bands,
-    base_ref,
-    mix_ref,
     scale_ref,
-    dep,
-    dual,
-    incr,
-    traj,
+    table_any,
+    mix_any,
+    dep_any,
+    dual_any,
+    incr_any,
+    traj_any,
+    spectrum_ref,
     innov,
     variance,
     held,
     time_ref,
     level_ref,
     point_ref,
+    dual_any_out,
+    out_held,
+    incr_any_out,
+    slid_any_out,
+    table,
+    mix_ref,
+    dep,
+    dual,
+    incr,
+    traj,
     out_dual,
-    out_held,
     out_incr,
-    out_slid,
     east,
     north,
     zonal_hi,
@@ -98,6 +107,8 @@
     slid_rsem,
     halo_ssem,
     halo_rsem,
+    load_sem,
+    store_sem,
 ):
     windows, levels, _, width = dep.shape
     obs = innov.shape[1]
@@ -110,8 +121,24 @@
     line = lax.broadcasted_iota(jnp.int32, (ROWS, width), 0)
     is_first, is_last = line == 0, line == ROWS - 1
 
+    loads = {}
+    for place, (name, source, target) in enumerate(
+        (
+            ("traj", traj_any, traj),
+            ("dual", dual_any, dual),
+            ("incr", incr_any, incr),
+            ("dep", dep_any, dep),
+            ("table", table_any, table),
+            ("mix", mix_any, mix_ref),
+        )
+    ):
+        loads[name] = pltpu.make_async_copy(source, target, load_sem.at[place])
+
     def both(*flags):
         return functools.reduce(jnp.logical_and, flags)
+
+    for name in ("traj", "dual", "incr"):
+        loads[name].start()
 
     barrier = pltpu.get_barrier_semaphore()
     around = ((0, None), (-1, has_below), (1, has_above))
@@ -337,8 +364,7 @@
         smooth = dot(high, zonal_hi[...]) + (dot(high, zonal_lo[...]) + dot(low, zonal_hi[...]))
         high, low = split(smooth)
         mixed = smooth + (dot(mix_hi[...], high) + (dot(mix_hi[...], low) + dot(mix_lo[...], high)))
-        scale = scale_ref[s]
-        target[s] = mixed * (scale * scale)
+        target[s] = mixed
 
     def first(lev):
         for s in (0, 1):
@@ -352,6 +378,10 @@
                 pulled[lev] = value
             edge_rows(2, s, lev, incr[s, lev])
 
+    for name in ("dep", "table", "mix"):
+        loads[name].start()
+    for name in ("traj", "dual", "incr"):
+        loads[name].wait()
     each_level(first)
     await_barrier()
 
@@ -372,8 +402,22 @@
     tables()
     spread(held)
 
-    def circulant(a, carry):
-        tall = [pltpu.roll(base_ref[...], a * 16 + t, 1) for t in (0, 8)]
+    def response():
+        modes = width // 2
+        row = jnp.broadcast_to(spectrum_ref[pl.ds(0, modes)].reshape(1, modes), (ROWS, modes))
+        high, low = split(row)
+        table_hi, table_lo = split(table[...])
+        first = dot(high, table_hi) + (dot(high, table_lo) + dot(low, table_hi))
+        cell = lax.broadcasted_iota(jnp.int32, (ROWS, width), 1)
+        parity = 1.0 - 2.0 * jnp.bitwise_and(cell, 1).astype(F32)
+        first = first + parity * (spectrum_ref[pl.ds(modes, 1)].reshape(1, 1) * (1.0 / width))
+        rows = first
+        for step in range(1, ROWS):
+            rows = jnp.where(line == step, pltpu.roll(first, step, 1), rows)
+        return rows
+
+    def circulant(rows, a, carry):
+        tall = [pltpu.roll(rows, a * 16 + t, 1) for t in (0, 8)]
         high, low = split(jnp.concatenate(tall, axis=0))
         at = pl.ds(pl.multiple_of(a * 16, 16), 16)
         zonal_hi[at, :] = high
@@ -407,7 +451,9 @@
     send_out(dual1, fore1, 0, 1)
     halo_start(1, 1)
 
-    lax.fori_loop(0, width // 16, circulant, 0)
+    for name in ("dep", "table", "mix"):
+        loads[name].wait()
+    lax.fori_loop(0, width // 16, functools.partial(circulant, response()), 0)
     mix_hi[...], mix_lo[...] = split(mix_ref[...])
     observe(incr, held, held1)
     spread(held1)
@@ -425,6 +471,8 @@
         out_dual[1, lev] = pull_recv[1, lev] + pulled_halo(1, 1, lev) - spread_ref[rows_of(levels + lev), :]
 
     each_level(dual2_next)
+    dual_store = pltpu.make_async_copy(out_dual, dual_any_out, store_sem.at[0])
+    dual_store.start()
     send_out(out_dual, fore2, 1, 1)
 
     for s in (0, 1):
@@ -451,7 +499,7 @@
         far_copy(mixed1, back1, 2, s).wait_recv()
 
         def incr1_of(lev, s=s):
-            field = part[s, lev] - back1[s, lev]
+            field = part[s, lev] - back1[s, lev] * (scale_ref[s] * scale_ref[s])
             incr1[s, lev] = field
             edge_rows(3, s, lev, field)
 
@@ -467,12 +515,18 @@
     observe(incr1, held1, out_held)
 
     def finish(s, lev, before):
-        field = dep[s, lev] + push(3, s, lev, before) - back2[s, lev]
+        field = dep[s, lev] + push(3, s, lev, before) - back2[s, lev] * (scale_ref[s] * scale_ref[s])
         out_incr[s, lev] = field
         slid_send[s, lev] = traj[s, lev] + field
 
     def slid_copy(s):
-        return remote(slid_send.at[s], out_slid.at[s], slid_ssem.at[s], slid_rsem.at[s], (grp - 1, me))
+        return remote(slid_send.at[s], slid_any_out.at[s], slid_ssem.at[s], slid_rsem.at[s], (grp - 1, me))
+
+    def incr_store(s):
+        return pltpu.make_async_copy(out_incr.at[s], incr_any_out.at[s], store_sem.at[1 + s])
+
+    def stay(s):
+        return pltpu.make_async_copy(slid_send.at[1], slid_any_out.at[s], store_sem.at[3 + s])
 
     for s in (1, 0):
         if s == 0:
@@ -485,13 +539,14 @@
         def _(s=s):
             slid_copy(s).start()
 
+        incr_store(s).start()
+
     @pl.when(jnp.logical_not(has_next))
     def _():
-        def stay(lev):
-            for s in (0, 1):
-                out_slid[s, lev] = slid_send[1, lev]
-
-        each_level(stay)
+        for s in (0, 1):
+            stay(s).start()
+        for s in (0, 1):
+            stay(s).wait()
 
     for s in (0, 1):
 
@@ -499,6 +554,9 @@
         def _(s=s):
             slid_copy(s).wait_recv()
 
+    dual_store.wait()
+    for s in (0, 1):
+        incr_store(s).wait()
     for s in (0, 1):
         far_copy(dual1, fore1, 0, s).wait_send()
         far_copy(out_dual, fore2, 1, s).wait_send()
@@ -525,13 +583,25 @@
         prior_copy(1, incr1).wait_send()
 
 
-def circulant_rows(spectrum, width):
-    modes, cells = np.arange(width // 2 + 1), np.arange(width)
-    weight = np.where((modes == 0) | (modes == width // 2), 1.0, 2.0) / width
+def cosine_table(width):
+    modes, cells = np.arange(width // 2), np.arange(width)
+    weight = np.where(modes == 0, 1.0, 2.0) / width
     angle = (modes[:, None] * cells[None, :] % width) * (2.0 * math.pi / width)
-    table = jnp.asarray((np.cos(angle) * weight[:, None]).astype(np.float32))
-    response = jnp.sum(table * spectrum[:, None], axis=0)
-    return jnp.stack([jnp.roll(response, i) for i in range(ROWS)])
+    return jnp.asarray((np.cos(angle) * weight[:, None]).astype(np.float32))
+
+
+def hand_over(count, *refs):
+    sources, targets, held = refs[:count], refs[count : 2 * count], refs[2 * count : 3 * count]
+    load_sem, store_sem = refs[3 * count :]
+    loads = [pltpu.make_async_copy(a, b, load_sem.at[i]) for i, (a, b) in enumerate(zip(sources, held))]
+    stores = [pltpu.make_async_copy(a, b, store_sem.at[i]) for i, (a, b) in enumerate(zip(held, targets))]
+    for load in loads:
+        load.start()
+    for load, store in zip(loads, stores):
+        load.wait()
+        store.start()
+    for store in stores:
+        store.wait()
 
 
 def on_device(
@@ -554,10 +624,11 @@
     lats = bands * rows
     obs = obs_dual.shape[0]
     cells = windows * levels * rows
-    base = circulant_rows(spectrum, width)
     flat = [v.reshape(1, obs) for v in (innovations, obs_variance, obs_dual, obs_time, obs_level, obs_point)]
     state = jax.ShapeDtypeStruct(increment.shape, F32)
+    held_shape = jax.ShapeDtypeStruct((1, obs), F32)
     vmem = pl.BlockSpec(memory_space=pltpu.VMEM)
+    anywhere = pl.BlockSpec(memory_space=pl.ANY)
     whole = pltpu.VMEM(increment.shape, F32)
     pencil = pltpu.VMEM((windows, lats, width), F32)
     window = pltpu.VMEM((levels, rows, width), F32)
@@ -566,10 +637,18 @@
     dma = pltpu.SemaphoreType.DMA
     dual, held, incr, slid = pl.pallas_call(
         functools.partial(kernel, groups, bands),
-        out_shape=(state, jax.ShapeDtypeStruct((1, obs), F32), state, state),
-        in_specs=[vmem, vmem, pl.BlockSpec(memory_space=pltpu.SMEM)] + [vmem] * 10,
-        out_specs=(vmem,) * 4,
+        out_shape=(state, held_shape, state, state),
+        in_specs=[pl.BlockSpec(memory_space=pltpu.SMEM)] + [anywhere] * 6 + [vmem] * 7,
+        out_specs=(anywhere, vmem, anywhere, anywhere),
         scratch_shapes=[
+            pltpu.VMEM((width // 2, width), F32),
+            pltpu.VMEM((lats, lats), F32),
+            whole,
+            whole,
+            whole,
+            whole,
+            whole,
+            whole,
             whole,
             whole,
             pltpu.VMEM((width, width), BF16),
@@ -609,20 +688,31 @@
             dma((2,)),
             dma((4, 2, 2)),
             dma((4, 2, 2)),
+            dma((6,)),
+            dma((5,)),
         ],
         compiler_params=pltpu.CompilerParams(
             collective_id=0, has_side_effects=True, vmem_limit_bytes=56 * 1024 * 1024
         ),
     )(
-        base,
+        error_scale,
+        cosine_table(width),
         lat_mix,
-        error_scale,
         departures,
         dual_state,
         increment,
         trajectory,
+        spectrum,
         *flat,
     )
+    memory = pl.BlockSpec(memory_space=pltpu.HBM)
+    dual, held, incr, slid = pl.pallas_call(
+        functools.partial(hand_over, 4),
+        out_shape=(state, held_shape, state, state),
+        in_specs=[memory] * 4,
+        out_specs=(memory,) * 4,
+        scratch_shapes=[whole, pltpu.VMEM((1, obs), F32), whole, whole, dma((4,)), dma((4,))],
+    )(dual, held, incr, slid)
     return (dual, held.reshape(obs), incr, slid)
 
 

time: 120 us -> 113 us (0.942)
  local copies, waits for them, and re-layouts: 7.87 us -> 0 us
  Pallas kernels: 109 us -> 112 us
  other arithmetic: 2.33 us -> 0 us
    unnamed x12 -> x0, local copies, waits for them, and re-layouts: 6.21 us -> none
    pallas_call x0 -> x1, Pallas kernels: none -> 2.96 us  [on_device(): pl.pallas_call(functools.partial(hand_over, 4), out_shape=(state, held_sh...]
where the time goes in v1:
time: 113 us
  Pallas kernels  112 us (99%)
    pallas_call x1, Pallas kernels, on_device(): pl.pallas_call(functools.partial(kernel, groups, bands), out_shape=(state...  109 us
    pallas_call x1, Pallas kernels, on_device(): pl.pallas_call(functools.partial(hand_over, 4), out_shape=(state, held_sh...  2.96 us

profile of v1, /device:TPU:1, one launch (start us, length us, event | category | flops | bytes accessed | tf_op | source)
XLA Modules:
  0.0 112.8 jit_solution(16411842943544056040)
XLA Ops:
  0.6 109.2 %shard_map.165 = (f32[2,32,8,512]{3,2,1,0:T(8,128)}, f32[1,4096]{1,0:T(1,128)}, f32[2,32,8,512]{3,2,1,0:T(8,128)}, f32[2,32,8,512]{3,2,1,0:T(8,128)}) custom-call(f32[2]{0:T(128)} %scale_ref.1, f32[256,512]{1,0:T(8,128)} %constant.2.clone.table_any, f32[256,256]{1,0:T(8,128)} %mix_any.1, f32[2,32,8,512]{3,2,1,0:T(8,128)} %dep_any.1, ...), custom_call_target="tpu_custom_call" | custom-call | tf_op jit(solution)/shard_map/pallas_call | solution.py:638
  109.8 3.0 %shard_map.166 = (f32[2,32,8,512]{3,2,1,0:T(8,128)}, f32[1,4096]{1,0:T(1,128)}, f32[2,32,8,512]{3,2,1,0:T(8,128)}, f32[2,32,8,512]{3,2,1,0:T(8,128)}) custom-call(f32[2,32,8,512]{3,2,1,0:T(8,128)} %get-tuple-element.12.refs_0_, f32[1,4096]{1,0:T(1,128)} %get-tuple-element.13.refs_1_, f32[2,32,8,512]{3,2,1,0:T(8,128)} %get-tuple-element.14.refs_2_, ...), custom_call_target="tpu_custom_call" | custom-call | tf_op jit(solution)/shard_map/pallas_call | solution.py:709

commit v2 on v1

--- a/solution.py
+++ b/solution.py
@@ -432,13 +432,13 @@
         pull_send[1, lev] = pull(1, 0, lev, field)
 
     each_level(dual1_here)
-    send_out(dual1, fore1, 0, 0)
 
     @pl.when(has_prev)
     def _():
         pull_copy(1).start()
 
     halo_start(1, 0)
+    send_out(dual1, fore1, 0, 0)
     hear_next(pull_copy(0), pull_recv.at[0])
     halo_wait(0, 1)
 
@@ -448,8 +448,8 @@
         pulled[lev] = pull(1, 1, lev, field)
 
     each_level(dual1_next)
+    halo_start(1, 1)
     send_out(dual1, fore1, 0, 1)
-    halo_start(1, 1)
 
     for name in ("dep", "table", "mix"):
         loads[name].wait()
@@ -490,10 +490,13 @@
 
     each_level(moved1)
 
-    for s in (0, 1):
-        far_copy(out_dual, fore2, 1, s).wait_recv()
-        cover(fore2, mixed2, s)
-        send_back(mixed2, back2, 3, s)
+    def second_filter():
+        for s in (0, 1):
+            far_copy(out_dual, fore2, 1, s).wait_recv()
+            cover(fore2, mixed2, s)
+            send_back(mixed2, back2, 3, s)
+
+    pl.when(grp == groups // 2)(second_filter)
 
     for s in (1, 0):
         far_copy(mixed1, back1, 2, s).wait_recv()
@@ -512,6 +515,7 @@
 
         halo_start(3, s)
 
+    pl.when(grp != groups // 2)(second_filter)
     observe(incr1, held1, out_held)
 
     def finish(s, lev, before):

time: 113 us -> 112 us (level)
    pallas_call x1, Pallas kernels: 109 us -> 108 us  [on_device(): pl.pallas_call(functools.partial(kernel, groups, bands), out_shape=(state...]
where the time goes in v2:
time: 112 us; the launch traced here: 111 us
  Pallas kernels  111 us (99%)
    pallas_call x1, Pallas kernels, on_device(): pl.pallas_call(functools.partial(kernel, groups, bands), out_shape=(state...  108 us
    pallas_call x1, Pallas kernels, on_device(): pl.pallas_call(functools.partial(hand_over, 4), out_shape=(state, held_sh...  2.96 us

profile of v2, /device:TPU:1, one launch (start us, length us, event | category | flops | bytes accessed | tf_op | source)
XLA Modules:
  0.0 111.4 jit_solution(1235872451109671703)
XLA Ops:
  0.6 107.8 %shard_map.165 = (f32[2,32,8,512]{3,2,1,0:T(8,128)}, f32[1,4096]{1,0:T(1,128)}, f32[2,32,8,512]{3,2,1,0:T(8,128)}, f32[2,32,8,512]{3,2,1,0:T(8,128)}) custom-call(f32[2]{0:T(128)} %scale_ref.1, f32[256,512]{1,0:T(8,128)} %constant.2.clone.table_any, f32[256,256]{1,0:T(8,128)} %mix_any.1, f32[2,32,8,512]{3,2,1,0:T(8,128)} %dep_any.1, ...), custom_call_target="tpu_custom_call" | custom-call | tf_op jit(solution)/shard_map/pallas_call | solution.py:642
  108.4 3.0 %shard_map.166 = (f32[2,32,8,512]{3,2,1,0:T(8,128)}, f32[1,4096]{1,0:T(1,128)}, f32[2,32,8,512]{3,2,1,0:T(8,128)}, f32[2,32,8,512]{3,2,1,0:T(8,128)}) custom-call(f32[2,32,8,512]{3,2,1,0:T(8,128)} %get-tuple-element.12.refs_0_, f32[1,4096]{1,0:T(1,128)} %get-tuple-element.13.refs_1_, f32[2,32,8,512]{3,2,1,0:T(8,128)} %get-tuple-element.14.refs_2_, ...), custom_call_target="tpu_custom_call" | custom-call | tf_op jit(solution)/shard_map/pallas_call | solution.py:713

commit v3 on v2

--- a/solution.py
+++ b/solution.py
@@ -113,7 +113,7 @@
     windows, levels, _, width = dep.shape
     obs = innov.shape[1]
     cells = windows * levels * ROWS
-    chunk = min(512, obs)
+    chunk = min(2048, obs)
     me = lax.axis_index("space")
     grp = lax.axis_index("tm")
     has_prev, has_next = grp > 0, grp < groups - 1
@@ -439,6 +439,10 @@
 
     halo_start(1, 0)
     send_out(dual1, fore1, 0, 0)
+    for name in ("dep", "table", "mix"):
+        loads[name].wait()
+    lax.fori_loop(0, width // 16, functools.partial(circulant, response()), 0)
+    mix_hi[...], mix_lo[...] = split(mix_ref[...])
     hear_next(pull_copy(0), pull_recv.at[0])
     halo_wait(0, 1)
 
@@ -451,10 +455,6 @@
     halo_start(1, 1)
     send_out(dual1, fore1, 0, 1)
 
-    for name in ("dep", "table", "mix"):
-        loads[name].wait()
-    lax.fori_loop(0, width // 16, functools.partial(circulant, response()), 0)
-    mix_hi[...], mix_lo[...] = split(mix_ref[...])
     observe(incr, held, held1)
     spread(held1)
     halo_wait(1, 0)
@@ -475,7 +475,7 @@
     dual_store.start()
     send_out(out_dual, fore2, 1, 1)
 
-    for s in (0, 1):
+    for s in (1, 0):
         far_copy(dual1, fore1, 0, s).wait_recv()
         cover(fore1, mixed1, s)
         send_back(mixed1, back1, 2, s)
@@ -491,12 +491,12 @@
     each_level(moved1)
 
     def second_filter():
-        for s in (0, 1):
+        for s in (1, 0):
             far_copy(out_dual, fore2, 1, s).wait_recv()
             cover(fore2, mixed2, s)
             send_back(mixed2, back2, 3, s)
 
-    pl.when(grp == groups // 2)(second_filter)
+    pl.when(grp <= groups // 2)(second_filter)
 
     for s in (1, 0):
         far_copy(mixed1, back1, 2, s).wait_recv()
@@ -515,8 +515,8 @@
 
         halo_start(3, s)
 
-    pl.when(grp != groups // 2)(second_filter)
     observe(incr1, held1, out_held)
+    pl.when(grp > groups // 2)(second_filter)
 
     def finish(s, lev, before):
         field = dep[s, lev] + push(3, s, lev, before) - back2[s, lev] * (scale_ref[s] * scale_ref[s])

time: 112 us -> 108 us (0.964)
  Pallas kernels: 111 us -> 107 us
    pallas_call x1, Pallas kernels: 108 us -> 104 us  [on_device(): pl.pallas_call(functools.partial(kernel, groups, bands), out_shape=(state...]
where the time goes in v3:
time: 108 us
  Pallas kernels  107 us (99%)
    pallas_call x1, Pallas kernels, on_device(): pl.pallas_call(functools.partial(kernel, groups, bands), out_shape=(state...  104 us
    pallas_call x1, Pallas kernels, on_device(): pl.pallas_call(functools.partial(hand_over, 4), out_shape=(state, held_sh...  2.96 us

profile of v3, /device:TPU:1, one launch (start us, length us, event | category | flops | bytes accessed | tf_op | source)
XLA Modules:
  0.0 107.7 jit_solution(247440750402090480)
XLA Ops:
  0.6 104.1 %shard_map.165 = (f32[2,32,8,512]{3,2,1,0:T(8,128)}, f32[1,4096]{1,0:T(1,128)}, f32[2,32,8,512]{3,2,1,0:T(8,128)}, f32[2,32,8,512]{3,2,1,0:T(8,128)}) custom-call(f32[2]{0:T(128)} %scale_ref.1, f32[256,512]{1,0:T(8,128)} %constant.2.clone.table_any, f32[256,256]{1,0:T(8,128)} %mix_any.1, f32[2,32,8,512]{3,2,1,0:T(8,128)} %dep_any.1, ...), custom_call_target="tpu_custom_call" | custom-call | tf_op jit(solution)/shard_map/pallas_call | solution.py:642
  104.7 3.0 %shard_map.166 = (f32[2,32,8,512]{3,2,1,0:T(8,128)}, f32[1,4096]{1,0:T(1,128)}, f32[2,32,8,512]{3,2,1,0:T(8,128)}, f32[2,32,8,512]{3,2,1,0:T(8,128)}) custom-call(f32[2,32,8,512]{3,2,1,0:T(8,128)} %get-tuple-element.12.refs_0_, f32[1,4096]{1,0:T(1,128)} %get-tuple-element.13.refs_1_, f32[2,32,8,512]{3,2,1,0:T(8,128)} %get-tuple-element.14.refs_2_, ...), custom_call_target="tpu_custom_call" | custom-call | tf_op jit(solution)/shard_map/pallas_call | solution.py:713

commit v4 on v3

--- a/solution.py
+++ b/solution.py
@@ -518,8 +518,11 @@
     observe(incr1, held1, out_held)
     pl.when(grp > groups // 2)(second_filter)
 
-    def finish(s, lev, before):
-        field = dep[s, lev] + push(3, s, lev, before) - back2[s, lev] * (scale_ref[s] * scale_ref[s])
+    def moved2(s, lev, before):
+        part[s, lev] = dep[s, lev] + push(3, s, lev, before)
+
+    def finish(s, lev):
+        field = part[s, lev] - back2[s, lev] * (scale_ref[s] * scale_ref[s])
         out_incr[s, lev] = field
         slid_send[s, lev] = traj[s, lev] + field
 
@@ -532,12 +535,15 @@
     def stay(s):
         return pltpu.make_async_copy(slid_send.at[1], slid_any_out.at[s], store_sem.at[3 + s])
 
+    halo_wait(3, 1)
+    each_level(lambda lev: moved2(1, lev, incr1[0, lev]))
     for s in (1, 0):
         if s == 0:
             hear_prev(prior_copy(1, incr1), prior.at[1])
-        halo_wait(3, s)
+            halo_wait(3, 0)
+            each_level(lambda lev: moved2(0, lev, prior[1, lev]))
         far_copy(mixed2, back2, 3, s).wait_recv()
-        each_level(lambda lev, s=s: finish(s, lev, prior[1, lev] if s == 0 else incr1[0, lev]))
+        each_level(functools.partial(finish, s))
 
         @pl.when(has_prev)
         def _(s=s):

time: 108 us -> 108 us (level)
  no operation moved by 1% of the time
where the time goes in v4:
time: 108 us
  Pallas kernels  107 us (99%)
    pallas_call x1, Pallas kernels, on_device(): pl.pallas_call(functools.partial(kernel, groups, bands), out_shape=(state...  104 us
    pallas_call x1, Pallas kernels, on_device(): pl.pallas_call(functools.partial(hand_over, 4), out_shape=(state, held_sh...  2.96 us

profile of v4, /device:TPU:1, one launch (start us, length us, event | category | flops | bytes accessed | tf_op | source)
XLA Modules:
  0.0 107.8 jit_solution(1973947603648255752)
XLA Ops:
  0.6 104.2 %shard_map.165 = (f32[2,32,8,512]{3,2,1,0:T(8,128)}, f32[1,4096]{1,0:T(1,128)}, f32[2,32,8,512]{3,2,1,0:T(8,128)}, f32[2,32,8,512]{3,2,1,0:T(8,128)}) custom-call(f32[2]{0:T(128)} %scale_ref.1, f32[256,512]{1,0:T(8,128)} %constant.2.clone.table_any, f32[256,256]{1,0:T(8,128)} %mix_any.1, f32[2,32,8,512]{3,2,1,0:T(8,128)} %dep_any.1, ...), custom_call_target="tpu_custom_call" | custom-call | tf_op jit(solution)/shard_map/pallas_call | solution.py:648
  104.8 3.0 %shard_map.166 = (f32[2,32,8,512]{3,2,1,0:T(8,128)}, f32[1,4096]{1,0:T(1,128)}, f32[2,32,8,512]{3,2,1,0:T(8,128)}, f32[2,32,8,512]{3,2,1,0:T(8,128)}) custom-call(f32[2,32,8,512]{3,2,1,0:T(8,128)} %get-tuple-element.12.refs_0_, f32[1,4096]{1,0:T(1,128)} %get-tuple-element.13.refs_1_, f32[2,32,8,512]{3,2,1,0:T(8,128)} %get-tuple-element.14.refs_2_, ...), custom_call_target="tpu_custom_call" | custom-call | tf_op jit(solution)/shard_map/pallas_call | solution.py:719
